TPU v7x, 32 devices: a whole 2x2x4 slice. The times are simulated.
32 devices in a mesh: tm: 8 (over y, x, core), space: 4 (over z).
Axes of the slice: x: 2, y: 2, z: 4, core: 2. Of those that a mesh axis runs over, the one named last changes fastest.
Arguments:
- queries: bfloat16 [8, 1024, 512], P('tm', 'space'), may hold values from -8 to 8
- key_tokens: bfloat16 [8, 1024, 512], P('tm', 'space'), may hold values from -8 to 8
- values: bfloat16 [8, 1024, 512], P('tm', 'space'), may hold values from -8 to 8
- near_list: int32 [8, 4, 8], replicated, may hold values from 0 to 11, as said below
- near_count: int32 [8, 4], replicated, may hold values from 1 to 8, as said below
- dist_band: int32 [8], replicated, may hold values from 0 to 3, as said below
- band_factor: int32 [3], replicated, may hold values from 1 to 4, as said below
Outputs:
- attended: bfloat16 [8, 1024, 512], P('tm', 'space')
Inputs may be any that keep to these rules, and one draw needn't show every extreme that they name: `near_list`: each entry is distinct within its list, never names a frame outside 0 to 7, and the first entry of block b is block b of the same frame. `near_count`: some query block of some frame lists 8 live blocks. `dist_band`: nondecreasing in the distance; 0 exactly for distances 0 and 1, 3 at distance 8 - 1. `band_factor`: each entry is 1, 2 or 4, and some entry is 4.
All inputs are finite; a program needn't handle non-finite values.
Results may differ from a plain program's by a relative error of at most 0.0028.
The roundings to bfloat16 on the way count: a program that leaves them out, or rounds other values in their place, can miss the bound.
Values may be sent and summed in bfloat16 or wider, within the bound.
A program may use at most 64 MiB of HBM per device.

v0:
```python
import math
import jax
import jax.numpy as jnp
from jax import lax
from jax.sharding import PartitionSpec as P

HD = 128
POOL = 128
lowest_score = -1e30


def extended(block, sides, width):
    for axis, dim in sides:
        count = lax.axis_size(axis)
        forward = [(i, i + 1) for i in range(count - 1)]
        backward = [(target, source) for source, target in forward]
        low = lax.ppermute(
            lax.slice_in_dim(block, block.shape[dim] - width, None, axis=dim), axis, forward
        )
        high = lax.ppermute(lax.slice_in_dim(block, 0, width, axis=dim), axis, backward)
        block = jnp.concatenate([low, block, high], axis=dim)
    return block


def lookup(table_values, positions):
    slot_ids = jnp.arange(table_values.shape[0], dtype=jnp.int32)
    picked = jnp.where(positions[:, None] == slot_ids[None, :], table_values[None, :], 0)
    return jnp.sum(picked, axis=1)


def coarsen(pooled, factor):
    frame_count, far_rows, head_count, head_size = pooled.shape
    widened = pooled.astype(jnp.float32)
    pair_means = jnp.mean(
        widened.reshape(frame_count, far_rows // 2, 2, head_count, head_size), axis=2
    ).astype(jnp.bfloat16)
    quad_means = jnp.mean(
        widened.reshape(frame_count, far_rows // 4, 4, head_count, head_size), axis=2
    ).astype(jnp.bfloat16)
    pair_means = jnp.repeat(pair_means, 2, axis=1)
    quad_means = jnp.repeat(quad_means, 4, axis=1)
    choose_factor = factor[:, None, None, None]
    return jnp.where(
        choose_factor == 1, pooled, jnp.where(choose_factor == 2, pair_means, quad_means)
    )


def attend_block(query_rows, near_k, near_v, near_ok, far_k, far_v, far_bias, far_ok):
    score_scale = 1.0 / math.sqrt(query_rows.shape[-1])
    near_scores = (
        jnp.einsum("bhd,khd->hbk", query_rows, near_k, preferred_element_type=jnp.float32)
        * score_scale
    )
    far_scores = (
        jnp.einsum("bhd,khd->hbk", query_rows, far_k, preferred_element_type=jnp.float32)
        * score_scale
        + far_bias[None, None, :]
    )
    near_scores = jnp.where(near_ok[None, None, :], near_scores, lowest_score)
    far_scores = jnp.where(far_ok[None, None, :], far_scores, lowest_score)
    row_top = jnp.maximum(
        jnp.max(near_scores, axis=-1, keepdims=True), jnp.max(far_scores, axis=-1, keepdims=True)
    )
    near_weights = jnp.where(near_ok[None, None, :], jnp.exp(near_scores - row_top), 0.0)
    far_weights = jnp.where(far_ok[None, None, :], jnp.exp(far_scores - row_top), 0.0)
    denominator = jnp.sum(near_weights, axis=-1) + jnp.sum(far_weights, axis=-1)
    weighted = jnp.einsum(
        "hbk,khd->bhd",
        near_weights.astype(jnp.bfloat16),
        near_v,
        preferred_element_type=jnp.float32,
    )
    weighted = weighted + jnp.einsum(
        "hbk,khd->bhd", far_weights.astype(jnp.bfloat16), far_v, preferred_element_type=jnp.float32
    )
    return (weighted / jnp.transpose(denominator)[:, :, None]).astype(jnp.bfloat16)


def attend_frame(
    query_frame,
    key_rim,
    value_rim,
    pooled_k,
    pooled_v,
    lists,
    counts,
    dist_band,
    band_factor,
    frame_index,
):
    frame_tokens, head_count, head_size = query_frame.shape
    block_count, list_length = lists.shape
    block_rows = frame_tokens // block_count
    frame_count, far_rows = (pooled_k.shape[0], pooled_k.shape[1])
    distance = jnp.abs(jnp.arange(frame_count, dtype=jnp.int32) - frame_index)
    band_index = lookup(dist_band, distance)
    factor = jnp.maximum(lookup(band_factor, band_index - 1), 1)
    far_k = coarsen(pooled_k, factor).reshape(frame_count * far_rows, head_count, head_size)
    far_v = coarsen(pooled_v, factor).reshape(frame_count * far_rows, head_count, head_size)
    far_bias = jnp.repeat(-jnp.log(factor.astype(jnp.float32)), far_rows)
    far_ok = jnp.repeat(distance >= 2, far_rows)
    key_blocks = key_rim.reshape(3 * block_count, block_rows, head_count, head_size)
    value_blocks = value_rim.reshape(3 * block_count, block_rows, head_count, head_size)

    def one_block(block_index):
        block_ids = lax.dynamic_index_in_dim(lists, block_index, 0, keepdims=False)
        live_slots = lax.dynamic_index_in_dim(counts, block_index, 0, keepdims=False)
        near_k = jnp.take(key_blocks, block_ids, axis=0).reshape(
            list_length * block_rows, head_count, head_size
        )
        near_v = jnp.take(value_blocks, block_ids, axis=0).reshape(
            list_length * block_rows, head_count, head_size
        )
        near_ok = jnp.repeat(jnp.arange(list_length, dtype=jnp.int32) < live_slots, block_rows)
        query_rows = lax.dynamic_slice_in_dim(query_frame, block_index * block_rows, block_rows, 0)
        return attend_block(query_rows, near_k, near_v, near_ok, far_k, far_v, far_bias, far_ok)

    results = lax.map(one_block, jnp.arange(block_count, dtype=jnp.int32))
    return results.reshape(frame_tokens, head_count, head_size)


def local(queries, key_tokens, values, near_list, near_count, dist_band, band_factor):
    tokens_dev = queries.shape[1]
    features = queries.shape[2]
    head_count = features // HD
    frame_index = lax.axis_index("tm")
    split_shape = (1, tokens_dev, head_count, HD)
    split_q, split_k, split_v = (
        lax.all_to_all(
            queries.reshape(split_shape), "space", split_axis=2, concat_axis=1, tiled=True
        ),
        lax.all_to_all(
            key_tokens.reshape(split_shape), "space", split_axis=2, concat_axis=1, tiled=True
        ),
        lax.all_to_all(
            values.reshape(split_shape), "space", split_axis=2, concat_axis=1, tiled=True
        ),
    )
    head_pair = jnp.stack([split_k, split_v], axis=1)
    rim_heads = extended(head_pair, (("tm", 0),), 1)
    key_rim = rim_heads[:, 0]
    value_rim = rim_heads[:, 1]
    frame_tokens = key_rim.shape[1]
    local_heads = key_rim.shape[2]
    own_pair = jnp.stack([key_rim[1], value_rim[1]], axis=0)
    pooled_heads = jnp.mean(
        own_pair.reshape(2, frame_tokens // POOL, POOL, local_heads, HD), axis=2, dtype=jnp.float32
    ).astype(jnp.bfloat16)
    far_pair = lax.all_gather(pooled_heads[None], "tm", axis=0, tiled=True)
    lists = lax.dynamic_index_in_dim(near_list, frame_index, 0, keepdims=False)
    counts = lax.dynamic_index_in_dim(near_count, frame_index, 0, keepdims=False)
    frame_output = attend_frame(
        split_q[0],
        key_rim,
        value_rim,
        far_pair[:, 0],
        far_pair[:, 1],
        lists,
        counts,
        dist_band,
        band_factor,
        frame_index,
    )
    returned = lax.all_to_all(frame_output[None], "space", split_axis=1, concat_axis=2, tiled=True)
    return returned.reshape(1, tokens_dev, features)


def solution(mesh):
    return jax.shard_map(
        local,
        mesh=mesh,
        in_specs=(
            P("tm", "space", None),
            P("tm", "space", None),
            P("tm", "space", None),
            P(),
            P(),
            P(),
            P(),
        ),
        out_specs=P("tm", "space", None),
        check_vma=False,
    )
```

profile of v0, /device:TPU:0, one launch (start us, length us, event | category | flops | bytes accessed | tf_op | source)
XLA Modules:
  0.0 123.3 jit_solution(3960450113721223402)
XLA Ops:
  0.0 1.8 %copy.51 = bf16[1,256,512]{1,2,0:T(8,128)(2,1)} copy(bf16[1,256,512]{2,1,0:T(8,128)(2,1)} %param.12) | data formatting | bytes 524288 | tf_op args[1]
  1.8 6.3 %all-to-all-start = ((bf16[1,256,4,128]{1,3,0,2:T(8,128)(2,1)}), bf16[1,256,4,128]{1,3,0,2:T(8,128)(2,1)S(1)}, u32[]{:S(2)}, u32[]{:S(2)}) async-start(bf16[1,256,4,128]{1,3,0,2:T(8,128)(2,1)} %bitcast.2), calls=%async_computation | async-start | bytes 524288 | tf_op jit(solution)/shard_map/all_to_all | solution.py:132
  10.1 1.8 %copy.54 = bf16[1,256,512]{1,2,0:T(8,128)(2,1)} copy(bf16[1,256,512]{2,1,0:T(8,128)(2,1)} %param.13) | data formatting | bytes 524288 | tf_op args[2]
  11.9 1.8 %copy.57 = bf16[1,256,512]{1,2,0:T(8,128)(2,1)} copy(bf16[1,256,512]{2,1,0:T(8,128)(2,1)} %param.11) | data formatting | bytes 524288 | tf_op args[0]
  13.8 3.2 %all-to-all-done = bf16[1,256,4,128]{1,3,0,2:T(8,128)(2,1)S(1)} async-done(((bf16[1,256,4,128]{1,3,0,2:T(8,128)(2,1)}), bf16[1,256,4,128]{1,3,0,2:T(8,128)(2,1)S(1)}, u32[]{:S(2)}, u32[]{:S(2)}) %all-to-all-start) | async-done | bytes 262176 | tf_op jit(solution)/shard_map/all_to_all | solution.py:132
  17.0 3.4 %all-to-all-start.1 = ((bf16[1,256,4,128]{1,3,0,2:T(8,128)(2,1)}), bf16[1,256,4,128]{1,3,0,2:T(8,128)(2,1)S(1)}, u32[]{:S(2)}, u32[]{:S(2)}) async-start(bf16[1,256,4,128]{1,3,0,2:T(8,128)(2,1)} %bitcast.7), calls=%async_computation.1 | async-start | bytes 524288 | tf_op jit(solution)/shard_map/all_to_all | solution.py:135
  20.7 6.8 %all-to-all-done.1 = bf16[1,256,4,128]{1,3,0,2:T(8,128)(2,1)S(1)} async-done(((bf16[1,256,4,128]{1,3,0,2:T(8,128)(2,1)}), bf16[1,256,4,128]{1,3,0,2:T(8,128)(2,1)S(1)}, u32[]{:S(2)}, u32[]{:S(2)}) %all-to-all-start.1) | async-done | bytes 262176 | tf_op jit(solution)/shard_map/all_to_all | solution.py:135
  27.5 3.4 %all-to-all-start.2 = ((bf16[1,256,4,128]{1,3,0,2:T(8,128)(2,1)}), bf16[1,256,4,128]{1,3,0,2:T(8,128)(2,1)S(1)}, u32[]{:S(2)}, u32[]{:S(2)}) async-start(bf16[1,256,4,128]{1,3,0,2:T(8,128)(2,1)} %bitcast.13), calls=%async_computation.2 | async-start | bytes 524288 | tf_op jit(solution)/shard_map/all_to_all | solution.py:129
  31.1 1.3 %collective-permute-start = (bf16[1,2,1024,1,128]{4,2,3,1,0:T(8,128)(2,1)S(1)}, bf16[1,2,1024,1,128]{4,2,3,1,0:T(8,128)(2,1)S(1)}, u32[]{:S(2)}, u32[]{:S(2)}) collective-permute-start(bf16[1,2,1024,1,128]{4,2,3,1,0:T(8,128)(2,1)S(1)} %pad_maximum_fusion.1), channel_id=1, source_target_pairs={{0,4},{4,8},{8,12},{12,16},{16,20},{20,24},{24,28},{1,5},{5,9},{9,... | collective-permute-start | bytes 1572872 | tf_op jit(solution)/shard_map/ppermute | solution.py:17
  32.4 1.3 %collective-permute-start.1 = (bf16[1,2,1024,1,128]{4,2,3,1,0:T(8,128)(2,1)S(1)}, bf16[1,2,1024,1,128]{4,2,3,1,0:T(8,128)(2,1)S(1)}, u32[]{:S(2)}, u32[]{:S(2)}) collective-permute-start(bf16[1,2,1024,1,128]{4,2,3,1,0:T(8,128)(2,1)S(1)} %pad_maximum_fusion.1), channel_id=1, source_target_pairs={{4,0},{8,4},{12,8},{16,12},{20,16},{24,20},{28,24},{5,1},{9,5},{13... | collective-permute-start | bytes 1572872 | tf_op jit(solution)/shard_map/ppermute | solution.py:20
  33.8 15.5 %all-gather = bf16[16,8,128]{2,1,0:T(8,128)(2,1)S(1)} all-gather(bf16[2,8,128]{2,1,0:T(8,128)(2,1)S(1)} %multiply_convert_fusion.4), channel_id=2, replica_groups=mesh['tm'=8,'space'=4] {'tm'}, dimensions={0}, use_global_device_ids=true | all-gather | bytes 36864 | tf_op jit(solution)/shard_map/all_gather | solution.py:149
  51.7 51.8 %while.11 = (s32[]{:T(128)}, bf16[4,256,1,128]{3,1,0,2:T(8,128)(2,1)}, s32[4]{0:T(128)S(1)}, s32[4,8]{1,0:T(4,128)S(1)}, bf16[12,256,1,128]{3,1,0,2:T(8,128)(2,1...) while((s32[]{:T(128)}, ...), condition=%wide.region_12.14_spmd.clone, body=%wide.region_7.13_spmd.clone.sunk | while | flops 282329664 | bytes 14615961 | solution.py:118
  54.3 1.8 %gather_fusion = bf16[8,256,128]{2,1,0:T(8,128)(2,1)S(1)} fusion(bf16[12,256,128]{2,1,0:T(8,128)(2,1)} %bitcast.129, s32[1024]{0:T(1024)S(1)} %pad_clamp_fusion.2), kind=kCustom, calls=%fused_computation.clone.clone.1 | custom fusion | bytes 1048608 | tf_op jit(solution)/shard_map/while/body/eval_jaxpr/jit(_take)/gather | solution.py:111
  59.8 1.4 %fusion.55 = (f32[256]{0:T(256)S(1)}, f32[256,2048]{1,0:T(8,128)S(1)}) fusion(bf16[2048,128]{1,0:T(8,128)(2,1)S(1)} %bitcast.134, bf16[1024,1,128]{2,0,1:T(8,128)(2,1)} %get-tuple-element.267, s32[]{:T(128)S(6)} %select_n.160, pred[2048]{0:T(1024)(128)(4,1)S(1)} %broadcast_in_dim.258), kind=kOutput, calls=%fused_computation.71.clone.1 | convolution fusion | flops 135790336 | bytes 2690052 | tf_op jit(solution)/shard_map/while/body/eval_jaxpr/bhd,khd->hbk/dot_general | solution.py:51
  67.3 1.8 %gather_fusion = bf16[8,256,128]{2,1,0:T(8,128)(2,1)S(1)} fusion(bf16[12,256,128]{2,1,0:T(8,128)(2,1)} %bitcast.129, s32[1024]{0:T(1024)S(1)} %pad_clamp_fusion.2), kind=kCustom, calls=%fused_computation.clone.clone.1 | custom fusion | bytes 1048608 | tf_op jit(solution)/shard_map/while/body/eval_jaxpr/jit(_take)/gather | solution.py:111
  72.7 1.4 %fusion.55 = (f32[256]{0:T(256)S(1)}, f32[256,2048]{1,0:T(8,128)S(1)}) fusion(bf16[2048,128]{1,0:T(8,128)(2,1)S(1)} %bitcast.134, bf16[1024,1,128]{2,0,1:T(8,128)(2,1)} %get-tuple-element.267, s32[]{:T(128)S(6)} %select_n.160, pred[2048]{0:T(1024)(128)(4,1)S(1)} %broadcast_in_dim.258), kind=kOutput, calls=%fused_computation.71.clone.1 | convolution fusion | flops 135790336 | bytes 2690052 | tf_op jit(solution)/shard_map/while/body/eval_jaxpr/bhd,khd->hbk/dot_general | solution.py:51
  80.3 1.8 %gather_fusion = bf16[8,256,128]{2,1,0:T(8,128)(2,1)S(1)} fusion(bf16[12,256,128]{2,1,0:T(8,128)(2,1)} %bitcast.129, s32[1024]{0:T(1024)S(1)} %pad_clamp_fusion.2), kind=kCustom, calls=%fused_computation.clone.clone.1 | custom fusion | bytes 1048608 | tf_op jit(solution)/shard_map/while/body/eval_jaxpr/jit(_take)/gather | solution.py:111
  85.7 1.4 %fusion.55 = (f32[256]{0:T(256)S(1)}, f32[256,2048]{1,0:T(8,128)S(1)}) fusion(bf16[2048,128]{1,0:T(8,128)(2,1)S(1)} %bitcast.134, bf16[1024,1,128]{2,0,1:T(8,128)(2,1)} %get-tuple-element.267, s32[]{:T(128)S(6)} %select_n.160, pred[2048]{0:T(1024)(128)(4,1)S(1)} %broadcast_in_dim.258), kind=kOutput, calls=%fused_computation.71.clone.1 | convolution fusion | flops 135790336 | bytes 2690052 | tf_op jit(solution)/shard_map/while/body/eval_jaxpr/bhd,khd->hbk/dot_general | solution.py:51
  93.2 1.8 %gather_fusion = bf16[8,256,128]{2,1,0:T(8,128)(2,1)S(1)} fusion(bf16[12,256,128]{2,1,0:T(8,128)(2,1)} %bitcast.129, s32[1024]{0:T(1024)S(1)} %pad_clamp_fusion.2), kind=kCustom, calls=%fused_computation.clone.clone.1 | custom fusion | bytes 1048608 | tf_op jit(solution)/shard_map/while/body/eval_jaxpr/jit(_take)/gather | solution.py:111
  98.7 1.4 %fusion.55 = (f32[256]{0:T(256)S(1)}, f32[256,2048]{1,0:T(8,128)S(1)}) fusion(bf16[2048,128]{1,0:T(8,128)(2,1)S(1)} %bitcast.134, bf16[1024,1,128]{2,0,1:T(8,128)(2,1)} %get-tuple-element.267, s32[]{:T(128)S(6)} %select_n.160, pred[2048]{0:T(1024)(128)(4,1)S(1)} %broadcast_in_dim.258), kind=kOutput, calls=%fused_computation.71.clone.1 | convolution fusion | flops 135790336 | bytes 2690052 | tf_op jit(solution)/shard_map/while/body/eval_jaxpr/bhd,khd->hbk/dot_general | solution.py:51
  100.4 1.0 fusion.54
  103.6 1.4 %copy.69 = bf16[1,1024,1,128]{3,2,0,1:T(2,128)(2,1)S(1)} copy(bf16[1,1024,1,128]{3,1,2,0:T(8,128)(2,1)} %bitcast.155) | data formatting | bytes 524288 | tf_op jit(solution)/shard_map/broadcast_in_dim;reshape | solution.py:164
  105.4 2.2 %reduce.19 = bf16[1024,128]{1,0:T(8,128)(2,1)S(1)} reduce(bf16[1024,1,1,128]{3,2,1,0:T(2,128)(2,1)S(1)} %bitcast.145, bf16[]{:T(256)} %broadcast.251), dimensions={1,2}, to_apply=%bitcast.101.reduce_sub_computation | reduce | bytes 524290
  107.7 14.2 %all_to_all.60 = bf16[4,2,16384]{2,1,0:T(2,128)(2,1)S(1)} all-to-all(bf16[4,2,16384]{2,1,0:T(2,128)(2,1)S(1)} %reshape.508), channel_id=1, replica_groups=mesh['tm'=8,'space'=4] {'space'}, dimensions={0} | all-to-all | bytes 524288 | tf_op jit(solution)/shard_map/all_to_all | solution.py:164
  (145 shorter events, 34.5 us)
Async XLA Ops:
  0.0 20.5 %copy-start = (s32[8,4,8]{2,1,0:T(4,128)S(1)}, s32[8,4,8]{2,1,0:T(4,128)}, u32[]{:S(2)}) copy-start(s32[8,4,8]{2,1,0:T(4,128)} %param.14) | copy-start | bytes 3076
  0.0 13.6 %copy-start.2 = (s32[8,4]{0,1:T(4,128)S(1)}, s32[8,4]{0,1:T(4,128)}, u32[]{:S(2)}) copy-start(s32[8,4]{0,1:T(4,128)} %param.15) | copy-start | bytes 388
  1.8 15.2 %all-to-all-start = ((bf16[1,256,4,128]{1,3,0,2:T(8,128)(2,1)}), bf16[1,256,4,128]{1,3,0,2:T(8,128)(2,1)S(1)}, u32[]{:S(2)}, u32[]{:S(2)}) async-start(bf16[1,256,4,128]{1,3,0,2:T(8,128)(2,1)} %bitcast.2), calls=%async_computation | async-start | bytes 524288 | tf_op jit(solution)/shard_map/all_to_all | solution.py:132
  17.0 10.4 %all-to-all-start.1 = ((bf16[1,256,4,128]{1,3,0,2:T(8,128)(2,1)}), bf16[1,256,4,128]{1,3,0,2:T(8,128)(2,1)S(1)}, u32[]{:S(2)}, u32[]{:S(2)}) async-start(bf16[1,256,4,128]{1,3,0,2:T(8,128)(2,1)} %bitcast.7), calls=%async_computation.1 | async-start | bytes 524288 | tf_op jit(solution)/shard_map/all_to_all | solution.py:135
  27.5 22.1 %all-to-all-start.2 = ((bf16[1,256,4,128]{1,3,0,2:T(8,128)(2,1)}), bf16[1,256,4,128]{1,3,0,2:T(8,128)(2,1)S(1)}, u32[]{:S(2)}, u32[]{:S(2)}) async-start(bf16[1,256,4,128]{1,3,0,2:T(8,128)(2,1)} %bitcast.13), calls=%async_computation.2 | async-start | bytes 524288 | tf_op jit(solution)/shard_map/all_to_all | solution.py:129
  31.1 19.4 %collective-permute-start = (bf16[1,2,1024,1,128]{4,2,3,1,0:T(8,128)(2,1)S(1)}, bf16[1,2,1024,1,128]{4,2,3,1,0:T(8,128)(2,1)S(1)}, u32[]{:S(2)}, u32[]{:S(2)}) collective-permute-start(bf16[1,2,1024,1,128]{4,2,3,1,0:T(8,128)(2,1)S(1)} %pad_maximum_fusion.1), channel_id=1, source_target_pairs={{0,4},{4,8},{8,12},{12,16},{16,20},{20,24},{24,28},{1,5},{5,9},{9,... | collective-permute-start | bytes 1572872 | tf_op jit(solution)/shard_map/ppermute | solution.py:17
  32.4 18.1 %collective-permute-start.1 = (bf16[1,2,1024,1,128]{4,2,3,1,0:T(8,128)(2,1)S(1)}, bf16[1,2,1024,1,128]{4,2,3,1,0:T(8,128)(2,1)S(1)}, u32[]{:S(2)}, u32[]{:S(2)}) collective-permute-start(bf16[1,2,1024,1,128]{4,2,3,1,0:T(8,128)(2,1)S(1)} %pad_maximum_fusion.1), channel_id=1, source_target_pairs={{4,0},{8,4},{12,8},{16,12},{20,16},{24,20},{28,24},{5,1},{9,5},{13... | collective-permute-start | bytes 1572872 | tf_op jit(solution)/shard_map/ppermute | solution.py:20
  61.2 2.2 %copy-start.1 = (bf16[8,256,1,128]{3,1,0,2:T(8,128)(2,1)S(1)}, bf16[8,256,1,128]{3,1,0,2:T(8,128)(2,1)}, u32[]{:S(2)}) copy-start(bf16[8,256,1,128]{3,1,0,2:T(8,128)(2,1)} %get-tuple-element.225) | copy-start | bytes 1572868 | tf_op jit(solution)/shard_map/while
  74.1 2.2 %copy-start.1 = (bf16[8,256,1,128]{3,1,0,2:T(8,128)(2,1)S(1)}, bf16[8,256,1,128]{3,1,0,2:T(8,128)(2,1)}, u32[]{:S(2)}) copy-start(bf16[8,256,1,128]{3,1,0,2:T(8,128)(2,1)} %get-tuple-element.225) | copy-start | bytes 1572868 | tf_op jit(solution)/shard_map/while
  87.1 2.2 %copy-start.1 = (bf16[8,256,1,128]{3,1,0,2:T(8,128)(2,1)S(1)}, bf16[8,256,1,128]{3,1,0,2:T(8,128)(2,1)}, u32[]{:S(2)}) copy-start(bf16[8,256,1,128]{3,1,0,2:T(8,128)(2,1)} %get-tuple-element.225) | copy-start | bytes 1572868 | tf_op jit(solution)/shard_map/while
  100.0 2.2 %copy-start.1 = (bf16[8,256,1,128]{3,1,0,2:T(8,128)(2,1)S(1)}, bf16[8,256,1,128]{3,1,0,2:T(8,128)(2,1)}, u32[]{:S(2)}) copy-start(bf16[8,256,1,128]{3,1,0,2:T(8,128)(2,1)} %get-tuple-element.225) | copy-start | bytes 1572868 | tf_op jit(solution)/shard_map/while
where the time goes:
time: 124 us; the launch traced here: 123 us
  local copies, waits for them, and re-layouts  30.9 us (25%)
  blocking collectives  29.7 us (24%)
  starting transfers between devices  15.7 us (13%)
  other arithmetic  13.3 us (11%)
  matrix products  12.8 us (10%)
  loops' own time  10.6 us (9%)
  waiting for transfers between devices  9.98 us (8%)
    all_gather x1, blocking collectives, local(): far_pair = lax.all_gather(pooled_heads[None], 'tm', axis=0, tiled=True)  15.5 us
    all_to_all x1, blocking collectives, local(): lax.all_to_all(frame_output[None], 'space', split_axis=1, concat_axis=2,...  14.2 us
    another operation x1, loops' own time, attend_frame(): results = lax.map(one_block, jnp.arange(block_count, dtype=jnp.int32))  10.6 us
    gather x4, local copies, waits for them, and re-layouts, one_block(): jnp.take(value_blocks, block_ids, axis=0)  7.12 us
    all_to_all x1, waiting for transfers between devices, local(): lax.all_to_all(values.reshape(split_shape), 'space', split_axis=2, concat...  6.76 us
    all_to_all x1, starting transfers between devices, local(): lax.all_to_all(key_tokens.reshape(split_shape), 'space', split_axis=2, co...  6.32 us
    unnamed x11, local copies, waits for them, and re-layouts  6.28 us
    dot_general x4, matrix products, attend_block(): jnp.einsum('bhd,khd->hbk', query_rows, near_k, preferred_element_type=jnp...  5.48 us
  transfers between devices with their start and end apart: 5, of which 2 were waited for; matrix products, arithmetic and copies ran while one was open for 6% of the time, Pallas kernels for 0%

commit v1 on v0

--- a/solution.py
+++ b/solution.py
@@ -161,7 +161,21 @@
         band_factor,
         frame_index,
     )
-    returned = lax.all_to_all(frame_output[None], "space", split_axis=1, concat_axis=2, tiled=True)
+    ways, here = (lax.axis_size("space"), lax.axis_index("space"))
+    width_2 = frame_output[None].shape[1] // ways
+    shape = list(frame_output[None].shape)
+    shape[1] = width_2
+    height = shape[2]
+    shape[2] = height * ways
+    full = jnp.zeros(shape, frame_output[None].dtype)
+    for mask in range(ways):
+        part = lax.dynamic_slice_in_dim(
+            frame_output[None], (here ^ mask) * width_2, width_2, axis=1
+        )
+        if mask:
+            part = lax.ppermute(part, "space", [(d, d ^ mask) for d in range(ways)])
+        full = lax.dynamic_update_slice_in_dim(full, part, (here ^ mask) * height, axis=2)
+    returned = full
     return returned.reshape(1, tokens_dev, features)
 
 

time: 124 us -> 120 us (0.968)
  blocking collectives: 29.7 us -> 15.5 us
  waiting for transfers between devices: 9.98 us -> 15.8 us
  starting transfers between devices: 15.7 us -> 20.3 us
  other arithmetic: 13.3 us -> 11.1 us
  local copies, waits for them, and re-layouts: 30.9 us -> 32.7 us
    all_to_all x1 -> x0, blocking collectives: 14.2 us -> none  [local(): lax.all_to_all(frame_output[None], 'space', split_axis=1, concat_axis=2,...]
    ppermute x0 -> x3, waiting for transfers between devices: none -> 5.83 us  [local(): part = lax.ppermute(part, 'space', [(d, d ^ mask) for d in range(ways)])]
    ppermute x0 -> x3, starting transfers between devices: none -> 4.51 us  [local(): part = lax.ppermute(part, 'space', [(d, d ^ mask) for d in range(ways)])]
    dynamic_update_slice x0 -> x4, local copies, waits for them, and re-layouts: none -> 3.04 us  [local(): lax.dynamic_update_slice_in_dim(full, part, (here ^ mask) * height, axis=2)]
    unnamed x1 -> x0, other arithmetic: 2.21 us -> none
    another operation x1 -> x0, local copies, waits for them, and re-layouts: 1.35 us -> none  [local(): frame_output[None]]
    unnamed x11 -> x7, local copies, waits for them, and re-layouts: 6.28 us -> 5.4 us
  transfers between devices with their start and end apart: 5 -> 8, of which waited for: 2 -> 5; matrix products, arithmetic and copies ran while one was open for 6% -> 6% of each run, Pallas kernels for 0% -> 0%
where the time goes in v1:
time: 120 us; the launch traced here: 119 us
  local copies, waits for them, and re-layouts  32.7 us (27%)
  starting transfers between devices  20.3 us (17%)
  waiting for transfers between devices  15.8 us (13%)
  blocking collectives  15.5 us (13%)
  matrix products  12.8 us (11%)
  other arithmetic  11.1 us (9%)
  loops' own time  10.6 us (9%)
    all_gather x1, blocking collectives, local(): far_pair = lax.all_gather(pooled_heads[None], 'tm', axis=0, tiled=True)  15.5 us
    another operation x1, loops' own time, attend_frame(): results = lax.map(one_block, jnp.arange(block_count, dtype=jnp.int32))  10.6 us
    gather x4, local copies, waits for them, and re-layouts, one_block(): jnp.take(value_blocks, block_ids, axis=0)  7.12 us
    all_to_all x1, waiting for transfers between devices, local(): lax.all_to_all(values.reshape(split_shape), 'space', split_axis=2, concat...  6.76 us
    all_to_all x1, starting transfers between devices, local(): lax.all_to_all(key_tokens.reshape(split_shape), 'space', split_axis=2, co...  6.32 us
    ppermute x3, waiting for transfers between devices, local(): part = lax.ppermute(part, 'space', [(d, d ^ mask) for d in range(ways)])  5.83 us
    dot_general x4, matrix products, attend_block(): jnp.einsum('bhd,khd->hbk', query_rows, near_k, preferred_element_type=jnp...  5.48 us
    unnamed x7, local copies, waits for them, and re-layouts  5.4 us
  transfers between devices with their start and end apart: 8, of which 5 were waited for; matrix products, arithmetic and copies ran while one was open for 6% of the time, Pallas kernels for 0%

profile of v1, /device:TPU:0, one launch (start us, length us, event | category | flops | bytes accessed | tf_op | source)
XLA Modules:
  0.0 118.9 jit_solution(4346282646402476084)
XLA Ops:
  0.0 1.8 %copy.52 = bf16[1,256,512]{1,2,0:T(8,128)(2,1)} copy(bf16[1,256,512]{2,1,0:T(8,128)(2,1)} %param.12) | data formatting | bytes 524288 | tf_op args[1]
  1.8 6.3 %all-to-all-start = ((bf16[1,256,4,128]{1,3,0,2:T(8,128)(2,1)}), bf16[1,256,4,128]{1,3,0,2:T(8,128)(2,1)S(1)}, u32[]{:S(2)}, u32[]{:S(2)}) async-start(bf16[1,256,4,128]{1,3,0,2:T(8,128)(2,1)} %bitcast.2), calls=%async_computation | async-start | bytes 524288 | tf_op jit(solution)/shard_map/all_to_all | solution.py:132
  10.1 1.8 %copy.55 = bf16[1,256,512]{1,2,0:T(8,128)(2,1)} copy(bf16[1,256,512]{2,1,0:T(8,128)(2,1)} %param.13) | data formatting | bytes 524288 | tf_op args[2]
  11.9 1.8 %copy.58 = bf16[1,256,512]{1,2,0:T(8,128)(2,1)} copy(bf16[1,256,512]{2,1,0:T(8,128)(2,1)} %param.11) | data formatting | bytes 524288 | tf_op args[0]
  13.9 3.2 %all-to-all-done = bf16[1,256,4,128]{1,3,0,2:T(8,128)(2,1)S(1)} async-done(((bf16[1,256,4,128]{1,3,0,2:T(8,128)(2,1)}), bf16[1,256,4,128]{1,3,0,2:T(8,128)(2,1)S(1)}, u32[]{:S(2)}, u32[]{:S(2)}) %all-to-all-start) | async-done | bytes 262176 | tf_op jit(solution)/shard_map/all_to_all | solution.py:132
  17.0 3.4 %all-to-all-start.1 = ((bf16[1,256,4,128]{1,3,0,2:T(8,128)(2,1)}), bf16[1,256,4,128]{1,3,0,2:T(8,128)(2,1)S(1)}, u32[]{:S(2)}, u32[]{:S(2)}) async-start(bf16[1,256,4,128]{1,3,0,2:T(8,128)(2,1)} %bitcast.7), calls=%async_computation.1 | async-start | bytes 524288 | tf_op jit(solution)/shard_map/all_to_all | solution.py:135
  20.7 6.8 %all-to-all-done.1 = bf16[1,256,4,128]{1,3,0,2:T(8,128)(2,1)S(1)} async-done(((bf16[1,256,4,128]{1,3,0,2:T(8,128)(2,1)}), bf16[1,256,4,128]{1,3,0,2:T(8,128)(2,1)S(1)}, u32[]{:S(2)}, u32[]{:S(2)}) %all-to-all-start.1) | async-done | bytes 262176 | tf_op jit(solution)/shard_map/all_to_all | solution.py:135
  27.5 3.4 %all-to-all-start.2 = ((bf16[1,256,4,128]{1,3,0,2:T(8,128)(2,1)}), bf16[1,256,4,128]{1,3,0,2:T(8,128)(2,1)S(1)}, u32[]{:S(2)}, u32[]{:S(2)}) async-start(bf16[1,256,4,128]{1,3,0,2:T(8,128)(2,1)} %bitcast.13), calls=%async_computation.2 | async-start | bytes 524288 | tf_op jit(solution)/shard_map/all_to_all | solution.py:129
  31.1 1.3 %collective-permute-start = (bf16[1,2,1024,1,128]{4,2,3,1,0:T(8,128)(2,1)S(1)}, bf16[1,2,1024,1,128]{4,2,3,1,0:T(8,128)(2,1)S(1)}, u32[]{:S(2)}, u32[]{:S(2)}) collective-permute-start(bf16[1,2,1024,1,128]{4,2,3,1,0:T(8,128)(2,1)S(1)} %pad_maximum_fusion.1), channel_id=1, source_target_pairs={{0,4},{4,8},{8,12},{12,16},{16,20},{20,24},{24,28},{1,5},{5,9},{9,... | collective-permute-start | bytes 1572872 | tf_op jit(solution)/shard_map/ppermute | solution.py:17
  32.4 1.3 %collective-permute-start.1 = (bf16[1,2,1024,1,128]{4,2,3,1,0:T(8,128)(2,1)S(1)}, bf16[1,2,1024,1,128]{4,2,3,1,0:T(8,128)(2,1)S(1)}, u32[]{:S(2)}, u32[]{:S(2)}) collective-permute-start(bf16[1,2,1024,1,128]{4,2,3,1,0:T(8,128)(2,1)S(1)} %pad_maximum_fusion.1), channel_id=1, source_target_pairs={{4,0},{8,4},{12,8},{16,12},{20,16},{24,20},{28,24},{5,1},{9,5},{13... | collective-permute-start | bytes 1572872 | tf_op jit(solution)/shard_map/ppermute | solution.py:20
  33.8 15.5 %all-gather = bf16[16,8,128]{2,1,0:T(8,128)(2,1)S(1)} all-gather(bf16[2,8,128]{2,1,0:T(8,128)(2,1)S(1)} %multiply_convert_fusion.4), channel_id=2, replica_groups=mesh['tm'=8,'space'=4] {'tm'}, dimensions={0}, use_global_device_ids=true | all-gather | bytes 36864 | tf_op jit(solution)/shard_map/all_gather | solution.py:149
  51.7 51.8 %while.11 = (s32[]{:T(128)}, bf16[4,256,1,128]{3,1,0,2:T(8,128)(2,1)}, s32[4]{0:T(128)S(1)}, s32[4,8]{1,0:T(4,128)S(1)}, bf16[12,256,1,128]{3,1,0,2:T(8,128)(2,1...) while((s32[]{:T(128)}, ...), condition=%wide.region_12.14_spmd.clone, body=%wide.region_7.13_spmd.clone.sunk | while | flops 282329664 | bytes 14615961 | solution.py:118
  54.3 1.8 %gather_fusion = bf16[8,256,128]{2,1,0:T(8,128)(2,1)S(1)} fusion(bf16[12,256,128]{2,1,0:T(8,128)(2,1)} %bitcast.121, s32[1024]{0:T(1024)S(1)} %pad_clamp_fusion.2), kind=kCustom, calls=%fused_computation.clone.clone.1 | custom fusion | bytes 1048608 | tf_op jit(solution)/shard_map/while/body/eval_jaxpr/jit(_take)/gather | solution.py:111
  59.8 1.4 %fusion.57 = (f32[256]{0:T(256)S(1)}, f32[256,2048]{1,0:T(8,128)S(1)}) fusion(bf16[2048,128]{1,0:T(8,128)(2,1)S(1)} %bitcast.126, bf16[1024,1,128]{2,0,1:T(8,128)(2,1)} %get-tuple-element.271, s32[]{:T(128)S(6)} %select_n.192, pred[2048]{0:T(1024)(128)(4,1)S(1)} %broadcast_in_dim.262), kind=kOutput, calls=%fused_computation.79.clone.1 | convolution fusion | flops 135790336 | bytes 2690052 | tf_op jit(solution)/shard_map/while/body/eval_jaxpr/bhd,khd->hbk/dot_general | solution.py:51
  67.3 1.8 %gather_fusion = bf16[8,256,128]{2,1,0:T(8,128)(2,1)S(1)} fusion(bf16[12,256,128]{2,1,0:T(8,128)(2,1)} %bitcast.121, s32[1024]{0:T(1024)S(1)} %pad_clamp_fusion.2), kind=kCustom, calls=%fused_computation.clone.clone.1 | custom fusion | bytes 1048608 | tf_op jit(solution)/shard_map/while/body/eval_jaxpr/jit(_take)/gather | solution.py:111
  72.7 1.4 %fusion.57 = (f32[256]{0:T(256)S(1)}, f32[256,2048]{1,0:T(8,128)S(1)}) fusion(bf16[2048,128]{1,0:T(8,128)(2,1)S(1)} %bitcast.126, bf16[1024,1,128]{2,0,1:T(8,128)(2,1)} %get-tuple-element.271, s32[]{:T(128)S(6)} %select_n.192, pred[2048]{0:T(1024)(128)(4,1)S(1)} %broadcast_in_dim.262), kind=kOutput, calls=%fused_computation.79.clone.1 | convolution fusion | flops 135790336 | bytes 2690052 | tf_op jit(solution)/shard_map/while/body/eval_jaxpr/bhd,khd->hbk/dot_general | solution.py:51
  80.3 1.8 %gather_fusion = bf16[8,256,128]{2,1,0:T(8,128)(2,1)S(1)} fusion(bf16[12,256,128]{2,1,0:T(8,128)(2,1)} %bitcast.121, s32[1024]{0:T(1024)S(1)} %pad_clamp_fusion.2), kind=kCustom, calls=%fused_computation.clone.clone.1 | custom fusion | bytes 1048608 | tf_op jit(solution)/shard_map/while/body/eval_jaxpr/jit(_take)/gather | solution.py:111
  85.7 1.4 %fusion.57 = (f32[256]{0:T(256)S(1)}, f32[256,2048]{1,0:T(8,128)S(1)}) fusion(bf16[2048,128]{1,0:T(8,128)(2,1)S(1)} %bitcast.126, bf16[1024,1,128]{2,0,1:T(8,128)(2,1)} %get-tuple-element.271, s32[]{:T(128)S(6)} %select_n.192, pred[2048]{0:T(1024)(128)(4,1)S(1)} %broadcast_in_dim.262), kind=kOutput, calls=%fused_computation.79.clone.1 | convolution fusion | flops 135790336 | bytes 2690052 | tf_op jit(solution)/shard_map/while/body/eval_jaxpr/bhd,khd->hbk/dot_general | solution.py:51
  93.2 1.8 %gather_fusion = bf16[8,256,128]{2,1,0:T(8,128)(2,1)S(1)} fusion(bf16[12,256,128]{2,1,0:T(8,128)(2,1)} %bitcast.121, s32[1024]{0:T(1024)S(1)} %pad_clamp_fusion.2), kind=kCustom, calls=%fused_computation.clone.clone.1 | custom fusion | bytes 1048608 | tf_op jit(solution)/shard_map/while/body/eval_jaxpr/jit(_take)/gather | solution.py:111
  98.7 1.4 %fusion.57 = (f32[256]{0:T(256)S(1)}, f32[256,2048]{1,0:T(8,128)S(1)}) fusion(bf16[2048,128]{1,0:T(8,128)(2,1)S(1)} %bitcast.126, bf16[1024,1,128]{2,0,1:T(8,128)(2,1)} %get-tuple-element.271, s32[]{:T(128)S(6)} %select_n.192, pred[2048]{0:T(1024)(128)(4,1)S(1)} %broadcast_in_dim.262), kind=kOutput, calls=%fused_computation.79.clone.1 | convolution fusion | flops 135790336 | bytes 2690052 | tf_op jit(solution)/shard_map/while/body/eval_jaxpr/bhd,khd->hbk/dot_general | solution.py:51
  104.6 2.0 %collective-permute-start.2 = (bf16[1,256,1,128]{3,1,2,0:T(8,128)(2,1)S(1)}, bf16[1,256,1,128]{3,1,2,0:T(8,128)(2,1)S(1)}, u32[]{:S(2)}, u32[]{:S(2)}) collective-permute-start(bf16[1,256,1,128]{3,1,2,0:T(8,128)(2,1)S(1)} %get-tuple-element.134), channel_id=1, source_target_pairs={{0,1},{1,0},{2,3},{3,2},{4,5},{5,4},{6,7},{7,6},{8,9},{9,8},{10,11... | collective-permute-start | bytes 196616 | tf_op jit(solution)/shard_map/ppermute | solution.py:176
  106.6 2.4 %collective-permute-start.3 = (bf16[1,256,1,128]{3,1,2,0:T(8,128)(2,1)S(1)}, bf16[1,256,1,128]{3,1,2,0:T(8,128)(2,1)S(1)}, u32[]{:S(2)}, u32[]{:S(2)}) collective-permute-start(bf16[1,256,1,128]{3,1,2,0:T(8,128)(2,1)S(1)} %get-tuple-element.133), channel_id=1, source_target_pairs={{0,2},{1,3},{2,0},{3,1},{4,6},{5,7},{6,4},{7,5},{8,10},{9,11},{10,... | collective-permute-start | bytes 196616 | tf_op jit(solution)/shard_map/ppermute | solution.py:176
  109.2 5.0 %collective-permute-done.3 = bf16[1,256,1,128]{3,1,2,0:T(8,128)(2,1)S(1)} collective-permute-done((bf16[1,256,1,128]{3,1,2,0:T(8,128)(2,1)S(1)}, bf16[1,256,1,128]{3,1,2,0:T(8,128)(2,1)S(1)}, u32[]{:S(2)}, u32[]{:S(2)}) %collective-permute-start.3) | collective-permute-done | bytes 65568 | tf_op jit(solution)/shard_map/ppermute | solution.py:176
  115.3 2.8 %dynamic_update_slice.19 = bf16[1,256,4,128]{3,2,1,0:T(4,128)(2,1)S(1)} dynamic-update-slice(bf16[1,256,4,128]{3,2,1,0:T(4,128)(2,1)S(1)} %copy.62, bf16[1,256,1,128]{3,2,1,0:T(2,128)(2,1)S(1)} %copy.63, s32[]{:T(128)} %constant.46.clone.1, s32[]{:T(128)} %constant.46.clone.1, s32[]{:T(128)S(6)} %select_n.143, s32[]{:T(128)} %constant.46.clone.1) | dynamic-update-slice | bytes 131076 | tf_op jit(solution)/shard_map/dynamic_update_slice | solution.py:177
  (150 shorter events, 36.6 us)
Async XLA Ops:
  0.0 20.5 %copy-start = (s32[8,4,8]{2,1,0:T(4,128)S(1)}, s32[8,4,8]{2,1,0:T(4,128)}, u32[]{:S(2)}) copy-start(s32[8,4,8]{2,1,0:T(4,128)} %param.14) | copy-start | bytes 3076
  0.0 13.7 %copy-start.2 = (s32[8,4]{0,1:T(4,128)S(1)}, s32[8,4]{0,1:T(4,128)}, u32[]{:S(2)}) copy-start(s32[8,4]{0,1:T(4,128)} %param.15) | copy-start | bytes 388
  1.8 15.2 %all-to-all-start = ((bf16[1,256,4,128]{1,3,0,2:T(8,128)(2,1)}), bf16[1,256,4,128]{1,3,0,2:T(8,128)(2,1)S(1)}, u32[]{:S(2)}, u32[]{:S(2)}) async-start(bf16[1,256,4,128]{1,3,0,2:T(8,128)(2,1)} %bitcast.2), calls=%async_computation | async-start | bytes 524288 | tf_op jit(solution)/shard_map/all_to_all | solution.py:132
  17.0 10.4 %all-to-all-start.1 = ((bf16[1,256,4,128]{1,3,0,2:T(8,128)(2,1)}), bf16[1,256,4,128]{1,3,0,2:T(8,128)(2,1)S(1)}, u32[]{:S(2)}, u32[]{:S(2)}) async-start(bf16[1,256,4,128]{1,3,0,2:T(8,128)(2,1)} %bitcast.7), calls=%async_computation.1 | async-start | bytes 524288 | tf_op jit(solution)/shard_map/all_to_all | solution.py:135
  27.5 22.1 %all-to-all-start.2 = ((bf16[1,256,4,128]{1,3,0,2:T(8,128)(2,1)}), bf16[1,256,4,128]{1,3,0,2:T(8,128)(2,1)S(1)}, u32[]{:S(2)}, u32[]{:S(2)}) async-start(bf16[1,256,4,128]{1,3,0,2:T(8,128)(2,1)} %bitcast.13), calls=%async_computation.2 | async-start | bytes 524288 | tf_op jit(solution)/shard_map/all_to_all | solution.py:129
  31.1 19.4 %collective-permute-start = (bf16[1,2,1024,1,128]{4,2,3,1,0:T(8,128)(2,1)S(1)}, bf16[1,2,1024,1,128]{4,2,3,1,0:T(8,128)(2,1)S(1)}, u32[]{:S(2)}, u32[]{:S(2)}) collective-permute-start(bf16[1,2,1024,1,128]{4,2,3,1,0:T(8,128)(2,1)S(1)} %pad_maximum_fusion.1), channel_id=1, source_target_pairs={{0,4},{4,8},{8,12},{12,16},{16,20},{20,24},{24,28},{1,5},{5,9},{9,... | collective-permute-start | bytes 1572872 | tf_op jit(solution)/shard_map/ppermute | solution.py:17
  32.4 18.1 %collective-permute-start.1 = (bf16[1,2,1024,1,128]{4,2,3,1,0:T(8,128)(2,1)S(1)}, bf16[1,2,1024,1,128]{4,2,3,1,0:T(8,128)(2,1)S(1)}, u32[]{:S(2)}, u32[]{:S(2)}) collective-permute-start(bf16[1,2,1024,1,128]{4,2,3,1,0:T(8,128)(2,1)S(1)} %pad_maximum_fusion.1), channel_id=1, source_target_pairs={{4,0},{8,4},{12,8},{16,12},{20,16},{24,20},{28,24},{5,1},{9,5},{13... | collective-permute-start | bytes 1572872 | tf_op jit(solution)/shard_map/ppermute | solution.py:20
  61.2 2.2 %copy-start.1 = (bf16[8,256,1,128]{3,1,0,2:T(8,128)(2,1)S(1)}, bf16[8,256,1,128]{3,1,0,2:T(8,128)(2,1)}, u32[]{:S(2)}) copy-start(bf16[8,256,1,128]{3,1,0,2:T(8,128)(2,1)} %get-tuple-element.229) | copy-start | bytes 1572868 | tf_op jit(solution)/shard_map/while
  74.1 2.2 %copy-start.1 = (bf16[8,256,1,128]{3,1,0,2:T(8,128)(2,1)S(1)}, bf16[8,256,1,128]{3,1,0,2:T(8,128)(2,1)}, u32[]{:S(2)}) copy-start(bf16[8,256,1,128]{3,1,0,2:T(8,128)(2,1)} %get-tuple-element.229) | copy-start | bytes 1572868 | tf_op jit(solution)/shard_map/while
  87.1 2.2 %copy-start.1 = (bf16[8,256,1,128]{3,1,0,2:T(8,128)(2,1)S(1)}, bf16[8,256,1,128]{3,1,0,2:T(8,128)(2,1)}, u32[]{:S(2)}) copy-start(bf16[8,256,1,128]{3,1,0,2:T(8,128)(2,1)} %get-tuple-element.229) | copy-start | bytes 1572868 | tf_op jit(solution)/shard_map/while
  100.0 2.2 %copy-start.1 = (bf16[8,256,1,128]{3,1,0,2:T(8,128)(2,1)S(1)}, bf16[8,256,1,128]{3,1,0,2:T(8,128)(2,1)}, u32[]{:S(2)}) copy-start(bf16[8,256,1,128]{3,1,0,2:T(8,128)(2,1)} %get-tuple-element.229) | copy-start | bytes 1572868 | tf_op jit(solution)/shard_map/while
  104.6 4.6 %collective-permute-start.2 = (bf16[1,256,1,128]{3,1,2,0:T(8,128)(2,1)S(1)}, bf16[1,256,1,128]{3,1,2,0:T(8,128)(2,1)S(1)}, u32[]{:S(2)}, u32[]{:S(2)}) collective-permute-start(bf16[1,256,1,128]{3,1,2,0:T(8,128)(2,1)S(1)} %get-tuple-element.134), channel_id=1, source_target_pairs={{0,1},{1,0},{2,3},{3,2},{4,5},{5,4},{6,7},{7,6},{8,9},{9,8},{10,11... | collective-permute-start | bytes 196616 | tf_op jit(solution)/shard_map/ppermute | solution.py:176
  106.6 7.6 %collective-permute-start.3 = (bf16[1,256,1,128]{3,1,2,0:T(8,128)(2,1)S(1)}, bf16[1,256,1,128]{3,1,2,0:T(8,128)(2,1)S(1)}, u32[]{:S(2)}, u32[]{:S(2)}) collective-permute-start(bf16[1,256,1,128]{3,1,2,0:T(8,128)(2,1)S(1)} %get-tuple-element.133), channel_id=1, source_target_pairs={{0,2},{1,3},{2,0},{3,1},{4,6},{5,7},{6,4},{7,5},{8,10},{9,11},{10,... | collective-permute-start | bytes 196616 | tf_op jit(solution)/shard_map/ppermute | solution.py:176
  109.0 6.2 %collective-permute-start.4 = (bf16[1,256,1,128]{3,1,2,0:T(8,128)(2,1)S(1)}, bf16[1,256,1,128]{3,1,2,0:T(8,128)(2,1)S(1)}, u32[]{:S(2)}, u32[]{:S(2)}) collective-permute-start(bf16[1,256,1,128]{3,1,2,0:T(8,128)(2,1)S(1)} %get-tuple-element.132), channel_id=1, source_target_pairs={{0,3},{1,2},{2,1},{3,0},{4,7},{5,6},{6,5},{7,4},{8,11},{9,10},{10,... | collective-permute-start | bytes 196616 | tf_op jit(solution)/shard_map/ppermute | solution.py:176
